TPU v7x, 256 devices: a whole 4x4x8 slice. The times are simulated.
256 devices in a mesh: pipe: 16 (over z_lo, x, core), expert: 16 (over z_hi, y).
Axes of the slice: x: 4, y: 4, z: 8 (z_hi: 4, z_lo: 2; z = z_hi * 2 + z_lo), core: 2. Of those that a mesh axis runs over, the one named last changes fastest.
Arguments:
- front_rows: bfloat16 [16, 1024, 3584], P('pipe', 'expert'), may hold values from -6 to 6
- front_grad: bfloat16 [16, 1024, 3584], P('pipe', 'expert'), may hold values from -6 to 6
- front_routes: int32 [16, 1024, 4], P('pipe', 'expert'), may hold values from 0 to 7, all different within a row; in each aligned block of 64 rows (0 to 63, 64 to 127, ..., all dimensions but the last counted through in order) at most 36 rows name the same one
- front_logits: bfloat16 [16, 1024, 4], P('pipe', 'expert'), may hold values from -6 to 6
- rear_rows: bfloat16 [16, 1024, 3584], P('pipe', 'expert'), may hold values from -6 to 6
- rear_grad: bfloat16 [16, 1024, 3584], P('pipe', 'expert'), may hold values from -6 to 6
- rear_routes: int32 [16, 1024, 4], P('pipe', 'expert'), may hold values from 0 to 7, all different within a row; in each aligned block of 64 rows (0 to 63, 64 to 127, ..., all dimensions but the last counted through in order) at most 36 rows name the same one
- rear_logits: bfloat16 [16, 1024, 4], P('pipe', 'expert'), may hold values from -6 to 6
- up_weight: bfloat16 [16, 3584, 8192], P('pipe', None, 'expert'), may hold values from -0.09375 to 0.09375
- down_weight: bfloat16 [16, 8192, 3584], P('pipe', 'expert'), may hold values from -0.1875 to 0.1875
Outputs:
- front_input_grad: bfloat16 [16, 1024, 3584], P('pipe', 'expert')
- rear_input_grad: bfloat16 [16, 1024, 3584], P('pipe', 'expert')
- down_grad: bfloat16 [16, 8192, 3584], P('pipe', 'expert')
Inputs may be any that keep to these rules, and one draw needn't show every extreme that they name: `front_routes`: each row names 4 different experts. In the rows of one device (aligned blocks of 64 rows within one pipe index), no expert is named by more than 36 rows, a bound that some block reaches. `rear_routes`: as for front_routes.
All inputs are finite; a program needn't handle non-finite values.
Results may differ from a plain program's by a relative error of at most 0.01.
Values may be sent and summed in bfloat16 or wider, within the bound.
A program may use at most 128 MiB of HBM per device.

v0:
```python
import functools

import jax
import jax.numpy as jnp
from jax import lax
from jax.experimental import pallas as pl
from jax.experimental.pallas import tpu as pltpu
from jax.sharding import PartitionSpec as P

EXPERTS = 8
CAP = 36
NY = 4
NZ = 4
TOK = 64
PAIR = 2 * TOK
SLOTS = 80
PAD = 128

epsilon = 1e-06
MESH = pl.DeviceIdType.MESH
F32, BF16 = jnp.float32, jnp.bfloat16

KEPT_UP, KEPT_DN, SWAP, SWAPPED_UP, SWAPPED_DN, FAR_KEPT, FAR_SWAPPED = range(7)
PACKED = 7
BACK = 11
SUM_FAR_KEPT, SUM_FAR_SWAPPED, SUM_ABOVE_KEPT, SUM_BELOW_SWAPPED, SUM_BELOW_KEPT, SUM_ABOVE_SWAPPED = range(15, 21)
RESULT = 21
UP_A, DOWN_A, UP_B, DOWN_B = range(22, 26)
MIRROR = 26


def gate_table(routes, logits):
    weights = jax.nn.sigmoid(logits.astype(F32))
    weights = (weights / jnp.sum(weights, axis=-1, keepdims=True)).astype(BF16)
    onehot = routes[..., None] == jnp.arange(EXPERTS, dtype=jnp.int32)
    picked = jnp.where(onehot, weights[..., None].astype(F32), F32(0.0))
    return jnp.sum(picked, axis=-2).astype(BF16)


def normalize(row_block):
    rows_float = row_block.astype(F32)
    inv_rms = lax.rsqrt(jnp.mean(rows_float * rows_float, axis=-1, keepdims=True) + epsilon)
    return (rows_float, inv_rms, (rows_float * inv_rms).astype(BF16))


def finish(rows_float, inv_rms, incoming, grad_normed):
    grad_normed = grad_normed.astype(F32)
    inner = jnp.sum(grad_normed * rows_float, axis=-1, keepdims=True) / rows_float.shape[-1]
    grad_rows = inv_rms * grad_normed - inv_rms * inv_rms * inv_rms * rows_float * inner
    return (incoming.astype(F32) + grad_rows).astype(BF16)


def tn(a, b):
    return lax.dot_general(a, b, (((0,), (0,)), ((), ())), preferred_element_type=F32)


def nt(a, b):
    return lax.dot_general(a, b, (((1,), (1,)), ((), ())), preferred_element_type=F32)


def nn(a, b):
    return lax.dot_general(a, b, (((1,), (0,)), ((), ())), preferred_element_type=F32)


def kernel(
    width, group, tile,
    kept, sent, up, down,
    out_kept, out_sent, out_down,
    tok, outbox, rows, hidden, grad_pre, picks, pieces, back, ret, retin, upw, dnw, part, mirror,
    send_sem, recv_sem, local_sem,
):
    tiles = width // tile
    pipe, place = lax.axis_index("pipe"), lax.axis_index("expert")
    core, y, z = pipe % 2, place % NY, place // NY
    served = ((y + 1) // 2) % 2
    stay = core == served
    leave = core != served
    mine, other = 2 * z + y // 2, 2 * z + 1 - y // 2
    twin = (pipe + 1 - 2 * core, place)
    beside = (pipe, z * NY + y + 1 - 2 * (y % 2))
    opposite = (pipe, z * NY + 3 - y)
    above = (pipe, ((z + 1) % NZ) * NY + y)
    below = (pipe, ((z + NZ - 1) % NZ) * NY + y)
    crossed = (twin[0], beside[1])

    barrier = pltpu.get_barrier_semaphore()
    for device in (twin, beside, opposite, above, below):
        pl.semaphore_signal(barrier, inc=1, device_id=device, device_id_type=MESH)

    @pl.when(leave)
    def _():
        pl.semaphore_signal(barrier, inc=1, device_id=crossed, device_id_type=MESH)
        pl.semaphore_wait(barrier, 6)

    @pl.when(stay)
    def _():
        pl.semaphore_wait(barrier, 5)

    def remote(index, src, dst, device):
        return pltpu.make_async_remote_copy(
            src_ref=src, dst_ref=dst, send_sem=send_sem.at[index], recv_sem=recv_sem.at[index],
            device_id=device, device_id_type=MESH,
        )

    first, second = pl.ds(0, TOK), pl.ds(TOK, TOK)
    copies = {
        KEPT_UP: remote(KEPT_UP, kept, tok.at[1, first], above),
        KEPT_DN: remote(KEPT_DN, kept, tok.at[1, second], below),
        SWAP: remote(SWAP, sent, tok.at[0, second], beside),
        SWAPPED_UP: remote(SWAPPED_UP, tok.at[0, second], tok.at[2, first], above),
        SWAPPED_DN: remote(SWAPPED_DN, tok.at[0, second], tok.at[2, second], below),
        FAR_KEPT: remote(FAR_KEPT, tok.at[1, first], tok.at[3, first], above),
        FAR_SWAPPED: remote(FAR_SWAPPED, tok.at[2, second], tok.at[3, second], below),
        SUM_FAR_KEPT: remote(SUM_FAR_KEPT, ret.at[0], retin.at[0], below),
        SUM_FAR_SWAPPED: remote(SUM_FAR_SWAPPED, ret.at[1], retin.at[1], above),
        SUM_ABOVE_KEPT: remote(SUM_ABOVE_KEPT, ret.at[2], retin.at[2], above),
        SUM_BELOW_SWAPPED: remote(SUM_BELOW_SWAPPED, ret.at[3], retin.at[3], below),
        SUM_BELOW_KEPT: remote(SUM_BELOW_KEPT, ret.at[4], retin.at[4], below),
        SUM_ABOVE_SWAPPED: remote(SUM_ABOVE_SWAPPED, ret.at[5], retin.at[5], above),
        RESULT: remote(RESULT, ret.at[6], out_sent, beside),
        UP_A: remote(UP_A, up, upw.at[0], crossed),
        DOWN_A: remote(DOWN_A, down, dnw.at[0], crossed),
        UP_B: remote(UP_B, upw.at[0], upw.at[1], twin),
        DOWN_B: remote(DOWN_B, dnw.at[0], dnw.at[1], twin),
    }
    for c in range(4):
        copies[PACKED + c] = remote(
            PACKED + c, outbox.at[pl.ds(c * SLOTS, SLOTS)], rows.at[pl.ds((2 * c + 1) * SLOTS, SLOTS)], opposite
        )
        copies[BACK + c] = remote(
            BACK + c, pieces.at[pl.ds((2 * c + 1) * SLOTS, SLOTS)], back.at[pl.ds(c * SLOTS, SLOTS)], opposite
        )
    sent_copies = []

    def start(index):
        copies[index].start()
        sent_copies.append(index)

    def arrived(index):
        copies[index].wait_recv()

    def columns(j):
        return pl.ds(pl.multiple_of(j * tile, tile), tile)

    def pack(c):
        table = tok[c, :, pl.ds(2 * width, PAD)].astype(F32)
        lane = lax.broadcasted_iota(jnp.int32, (PAIR, PAD), 1)
        later = jnp.where(lax.broadcasted_iota(jnp.int32, (PAIR, 1), 0) >= TOK, F32(CAP), F32(0.0))
        plain, weighted = [], []
        for expert in (mine, other):
            gate = jnp.sum(jnp.where(lane == expert, table, 0.0), axis=1, keepdims=True)
            rank = jnp.sum(jnp.where(lane == expert + EXPERTS, table, 0.0), axis=1, keepdims=True) + later
            hit = (gate != 0.0) & (rank == lane.astype(F32))
            plain.append(jnp.where(hit, 1.0, 0.0).astype(BF16))
            weighted.append(jnp.where(hit, gate, 0.0).astype(BF16))
        plain, weighted = jnp.concatenate(plain, axis=1), jnp.concatenate(weighted, axis=1)
        picks[c] = plain
        for part_of, matrix in ((0, plain), (width, weighted)):

            def body(j, _, part_of=part_of, matrix=matrix):
                where = pl.ds(pl.multiple_of(part_of + j * tile, 128), tile)
                got = tn(matrix, tok[c, :, where]).astype(BF16)
                rows[pl.ds(2 * c * SLOTS, SLOTS), where] = got[:SLOTS]
                outbox[pl.ds(c * SLOTS, SLOTS), where] = got[PAD : PAD + SLOTS]
                return 0

            lax.fori_loop(0, tiles, body, 0)

    def expert(c):
        block = pl.ds(2 * c * SLOTS, 2 * SLOTS)

        def half(g, _):
            where = pl.ds(pl.multiple_of(g * group, group), group)
            pre = nn(rows[block, pl.ds(0, width)], upw[g])
            s = jax.nn.sigmoid(pre)
            hidden[block, where] = (pre * s).astype(BF16)
            grad_hidden = nt(rows[block, pl.ds(width, width)], dnw[g])
            grad_pre[:, where] = (grad_hidden * s * (1.0 + pre * (1.0 - s))).astype(BF16)
            return 0

        lax.fori_loop(0, 2, half, 0)

        def body(j, _):
            where = columns(j)
            total = nt(grad_pre[:, pl.ds(0, group)], upw[0, where, :]) + nt(
                grad_pre[:, pl.ds(group, group)], upw[1, where, :]
            )
            pieces[block, where] = total.astype(BF16)
            return 0

        lax.fori_loop(0, tiles, body, 0)

    def scatter(c, half, extras, store):
        tokens = pl.ds(half * TOK, TOK)

        def body(j, _):
            where = columns(j)
            total = nn(picks[c, tokens, pl.ds(0, SLOTS)], pieces[pl.ds(2 * c * SLOTS, SLOTS), where])
            total += nn(picks[c, tokens, pl.ds(PAD, SLOTS)], back[pl.ds(c * SLOTS, SLOTS), where])
            for extra in extras:
                total += retin[extra, :, where].astype(F32)
            ret[store, :, where] = total.astype(BF16)
            return 0

        lax.fori_loop(0, tiles, body, 0)

    start(KEPT_UP)
    start(KEPT_DN)
    start(SWAP)
    own = pltpu.make_async_copy(kept, tok.at[0, first], local_sem.at[0])
    own.start()

    @pl.when(stay)
    def _():
        one = pltpu.make_async_copy(up, upw.at[0], local_sem.at[1])
        two = pltpu.make_async_copy(down, dnw.at[0], local_sem.at[2])
        one.start()
        two.start()
        one.wait()
        two.wait()
        copies[UP_B].start()
        copies[DOWN_B].start()

    arrived(SWAP)
    start(SWAPPED_UP)
    start(SWAPPED_DN)

    @pl.when(leave)
    def _():
        copies[UP_A].start()
        copies[DOWN_A].start()

    own.wait()
    pack(0)
    start(PACKED)
    arrived(KEPT_UP)
    start(FAR_KEPT)
    arrived(KEPT_DN)
    pack(1)
    start(PACKED + 1)
    arrived(SWAPPED_DN)
    start(FAR_SWAPPED)
    arrived(SWAPPED_UP)
    pack(2)
    start(PACKED + 2)

    @pl.when(leave)
    def _():
        copies[UP_A].wait()
        copies[DOWN_A].wait()
        copies[UP_B].start()
        copies[DOWN_B].start()

    sent_copies.extend([UP_B, DOWN_B])
    arrived(UP_B)
    arrived(DOWN_B)
    arrived(PACKED)
    expert(0)
    start(BACK)
    arrived(FAR_KEPT)
    arrived(FAR_SWAPPED)
    pack(3)
    start(PACKED + 3)
    arrived(PACKED + 1)
    expert(1)
    start(BACK + 1)
    arrived(PACKED + 2)
    expert(2)
    start(BACK + 2)
    arrived(BACK + 1)
    scatter(1, 1, (), 2)
    start(SUM_ABOVE_KEPT)
    arrived(BACK + 2)
    scatter(2, 0, (), 3)
    start(SUM_BELOW_SWAPPED)
    arrived(PACKED + 3)
    expert(3)
    start(BACK + 3)

    def mirrored(j):
        return pltpu.make_async_remote_copy(
            src_ref=part.at[:, columns(j)], dst_ref=mirror.at[:, columns(j)],
            send_sem=send_sem.at[MIRROR + j], recv_sem=recv_sem.at[MIRROR + j],
            device_id=twin, device_id_type=MESH,
        )

    def home(j):
        return pltpu.make_async_remote_copy(
            src_ref=mirror.at[:, columns(j)], dst_ref=out_down.at[:, columns(j)],
            send_sem=send_sem.at[MIRROR + tiles + j], recv_sem=recv_sem.at[MIRROR + tiles + j],
            device_id=crossed, device_id_type=MESH,
        )

    def stays(j):
        return pltpu.make_async_copy(
            mirror.at[:, columns(j)], out_down.at[:, columns(j)], local_sem.at[3 + j]
        )

    def gradient(j, g):
        where = pl.ds(pl.multiple_of(width + j * tile, 128), tile)
        return tn(hidden[:, pl.ds(g * group, group)], rows[:, where])

    def theirs(j, _):
        part[:, columns(j)] = gradient(j, 1).astype(BF16)
        mirrored(j).start()
        return 0

    lax.fori_loop(0, tiles, theirs, 0)

    arrived(BACK + 3)
    scatter(3, 0, (), 0)
    start(SUM_FAR_KEPT)
    scatter(3, 1, (), 1)
    start(SUM_FAR_SWAPPED)

    def ours(j, _):
        value = gradient(j, 0).astype(BF16).astype(F32)
        mirrored(j).wait_recv()
        mirror[:, columns(j)] = (value + mirror[:, columns(j)].astype(F32)).astype(BF16)

        @pl.when(stay)
        def _():
            stays(j).start()

        @pl.when(leave)
        def _():
            home(j).start()

        return 0

    lax.fori_loop(0, tiles, ours, 0)

    arrived(SUM_FAR_KEPT)
    scatter(1, 0, (0,), 4)
    start(SUM_BELOW_KEPT)
    arrived(SUM_FAR_SWAPPED)
    scatter(2, 1, (1,), 5)
    start(SUM_ABOVE_SWAPPED)
    arrived(BACK)
    arrived(SUM_BELOW_SWAPPED)
    arrived(SUM_ABOVE_SWAPPED)
    scatter(0, 1, (3, 5), 6)
    start(RESULT)
    arrived(SUM_ABOVE_KEPT)
    arrived(SUM_BELOW_KEPT)
    scatter(0, 0, (2, 4), 7)
    result = pltpu.make_async_copy(ret.at[7], out_kept, local_sem.at[0])
    result.start()

    for index in sent_copies:
        copies[index].wait_send()

    def ended(j, _):
        mirrored(j).wait_send()

        @pl.when(stay)
        def _():
            stays(j).wait()

        @pl.when(leave)
        def _():
            home(j).wait()

        return 0

    lax.fori_loop(0, tiles, ended, 0)
    result.wait()
    arrived(RESULT)


def exchange(kept, sent, up, down):
    width, group = up.shape
    tile = 512 if width % 512 == 0 else 128
    tiles = width // tile
    copies = MIRROR + 2 * tiles
    return pl.pallas_call(
        functools.partial(kernel, width, group, tile),
        out_shape=[
            jax.ShapeDtypeStruct((TOK, width), BF16),
            jax.ShapeDtypeStruct((TOK, width), BF16),
            jax.ShapeDtypeStruct((group, width), BF16),
        ],
        in_specs=[pl.BlockSpec(memory_space=pl.ANY)] * 4,
        out_specs=[pl.BlockSpec(memory_space=pl.ANY)] * 3,
        scratch_shapes=[
            pltpu.VMEM((4, PAIR, 2 * width + PAD), BF16),
            pltpu.VMEM((4 * SLOTS, 2 * width), BF16),
            pltpu.VMEM((8 * SLOTS, 2 * width), BF16),
            pltpu.VMEM((8 * SLOTS, 2 * group), BF16),
            pltpu.VMEM((2 * SLOTS, 2 * group), BF16),
            pltpu.VMEM((4, PAIR, 2 * PAD), BF16),
            pltpu.VMEM((8 * SLOTS, width), BF16),
            pltpu.VMEM((4 * SLOTS, width), BF16),
            pltpu.VMEM((8, TOK, width), BF16),
            pltpu.VMEM((6, TOK, width), BF16),
            pltpu.VMEM((2, width, group), BF16),
            pltpu.VMEM((2, group, width), BF16),
            pltpu.VMEM((group, width), BF16),
            pltpu.VMEM((group, width), BF16),
            pltpu.SemaphoreType.DMA((copies,)),
            pltpu.SemaphoreType.DMA((copies,)),
            pltpu.SemaphoreType.DMA((3 + tiles,)),
        ],
        compiler_params=pltpu.CompilerParams(
            collective_id=0, has_side_effects=True, vmem_limit_bytes=62 * 1024 * 1024
        ),
    )(kept, sent, up, down)


def on_device(fx, fg, froutes, flogits, rx, rg, rroutes, rlogits, up_weight, down_weight):
    core = lax.axis_index("pipe") % 2
    y = lax.axis_index("expert") % NY
    front_stays = core == (y + 1) // 2 % 2
    both = []
    for x, g, routes, logits in ((fx, fg, froutes, flogits), (rx, rg, rroutes, rlogits)):
        rows_float, inv_rms, normed = normalize(x[0])
        gates = gate_table(routes[0], logits[0])
        chosen = (gates != 0).astype(jnp.int32)
        rank = (jnp.cumsum(chosen, axis=0) - chosen).astype(BF16)
        table = jnp.pad(jnp.concatenate([gates, rank], axis=1), ((0, 0), (0, PAD - 2 * EXPERTS)))
        both.append((rows_float, inv_rms, g[0], jnp.concatenate([normed, g[0], table], axis=1)))
    kept = jnp.where(front_stays, both[0][3], both[1][3])
    sent = jnp.where(front_stays, both[1][3], both[0][3])
    from_kept, from_sent, down_grad = exchange(kept, sent, up_weight[0], down_weight[0])
    results = []
    for stays, (rows_float, inv_rms, g, _) in zip((front_stays, ~front_stays), both):
        results.append(finish(rows_float, inv_rms, g, jnp.where(stays, from_kept, from_sent)))
    return (results[0][None], results[1][None], down_grad[None])


def solution(mesh):
    rows = P("pipe", "expert", None)
    return jax.shard_map(
        on_device,
        mesh=mesh,
        in_specs=(rows,) * 8 + (P("pipe", None, "expert"), rows),
        out_specs=(rows, rows, rows),
        check_vma=False,
    )
```

profile of v0, /device:TPU:36, one launch (start us, length us, event | category | flops | bytes accessed | tf_op | source)
XLA Modules:
  0.0 291.6 jit_solution(18179659002996412363)
XLA Ops:
  0.6 0.0 copy-start
  0.7 0.0 copy-start.1
  0.7 0.8 fusion.26
  1.6 0.7 fusion.29
  2.3 0.7 select_reduce_fusion.1
  3.0 0.1 copy.27
  3.1 0.1 reduce_window_sum.17
  3.2 0.7 fusion.27
  3.9 0.7 fusion.28
  4.6 0.7 select_reduce_fusion
  5.3 0.1 copy.28
  5.4 0.1 reduce_window_sum.18
  5.5 0.1 fusion.20
  5.6 1.2 fusion.6
  6.8 1.2 fusion.10
  8.1 0.2 fusion.7
  8.3 1.5 broadcast_select_fusion
  9.9 275.8 %shard_map.121 = (bf16[64,3584]{1,0:T(8,128)(2,1)}, bf16[64,3584]{1,0:T(8,128)(2,1)}, bf16[512,3584]{1,0:T(8,128)(2,1)}) custom-call(bf16[64,7296]{1,0:T(8,128)(2,1)} %get-tuple-element.12.kept, bf16[64,7296]{1,0:T(8,128)(2,1)} %get-tuple-element.11.sent, bf16[3584,512]{1,0:T(8,128)(2,1)} %bitcast.47, bf16[512,3584]{1,0:T(8,128)(2,1)} %bitcast.48), custom_call_target="tpu_custom_call" | custom-call | tf_op jit(solution)/shard_map/pallas_call | solution.py:376
  285.7 1.6 fusion.13
  287.4 0.0 copy-done.3
  287.4 0.0 copy-done.4
  287.4 1.6 fusion.14
  289.0 0.7 copy-done.2
  289.7 1.8 copy.30
  (17 shorter events, 0.1 us)
Async XLA Ops:
  0.6 7.4 %copy-start = (bf16[1,64,3584]{2,1,0:T(8,128)(2,1)S(1)}, bf16[1,64,3584]{2,1,0:T(8,128)(2,1)}, u32[]{:S(2)}) copy-start(bf16[1,64,3584]{2,1,0:T(8,128)(2,1)} %param.14) | copy-start | bytes 1376260
  0.6 7.7 %copy-start.5 = (bf16[1,64,3584]{2,1,0:T(8,128)(2,1)S(1)}, bf16[1,64,3584]{2,1,0:T(8,128)(2,1)}, u32[]{:S(2)}) copy-start(bf16[1,64,3584]{2,1,0:T(8,128)(2,1)} %param.15) | copy-start | bytes 1376260
  0.7 7.4 %copy-start.1 = (bf16[1,64,3584]{2,1,0:T(8,128)(2,1)S(1)}, bf16[1,64,3584]{2,1,0:T(8,128)(2,1)}, u32[]{:S(2)}) copy-start(bf16[1,64,3584]{2,1,0:T(8,128)(2,1)} %param.10) | copy-start | bytes 1376260
  0.7 7.6 %copy-start.6 = (bf16[1,64,3584]{2,1,0:T(8,128)(2,1)S(1)}, bf16[1,64,3584]{2,1,0:T(8,128)(2,1)}, u32[]{:S(2)}) copy-start(bf16[1,64,3584]{2,1,0:T(8,128)(2,1)} %param.11) | copy-start | bytes 1376260
  285.7 1.7 copy-start.3
  285.7 1.7 copy-start.4
  287.3 2.4 copy-start.2
where the time goes:
time: 292 us
  Pallas kernels  276 us (95%)
  other arithmetic  12.1 us (4%)
    pallas_call x1, Pallas kernels, exchange(): pl.pallas_call(functools.partial(kernel, width, group, tile), out_shape=[...  276 us

commit v1 on v0

v1 whole, which is shorter than its diff:
```python
import functools

import jax
import jax.numpy as jnp
from jax import lax
from jax.experimental import pallas as pl
from jax.experimental.pallas import tpu as pltpu
from jax.sharding import PartitionSpec as P

EXPERTS = 8
CAP = 36
NY = 4
NZ = 4
TOK = 64
PAIR = 2 * TOK
SLOTS = 80
PAD = 128

epsilon = 1e-06
MESH = pl.DeviceIdType.MESH
F32, BF16 = jnp.float32, jnp.bfloat16

(
    KEPT_UP, KEPT_DN, SWAPPED_UP, SWAPPED_DN, FAR_UP, FAR_DN, SWAP, PACKED, _PACKED_1, _PACKED_2, _PACKED_3, PARTS,
) = range(12)
UP_A, DOWN_A, UP_B, DOWN_B = range(2 * PARTS, 2 * PARTS + 4)
TILED = 2 * PARTS + 4
SUM_FAR_KEPT, SUM_FAR_SWAPPED, SUM_ABOVE_KEPT, SUM_BELOW_SWAPPED, SUM_BELOW_KEPT, SUM_ABOVE_SWAPPED = range(6)
RESULT = 6
BACK = 7
MIRROR = 11
HOME = 12
TILED_KINDS = 13


def gate_table(routes, logits):
    weights = jax.nn.sigmoid(logits.astype(F32))
    weights = (weights / jnp.sum(weights, axis=-1, keepdims=True)).astype(BF16)
    onehot = routes[..., None] == jnp.arange(EXPERTS, dtype=jnp.int32)
    picked = jnp.where(onehot, weights[..., None].astype(F32), F32(0.0))
    return jnp.sum(picked, axis=-2).astype(BF16)


def normalize(row_block):
    rows_float = row_block.astype(F32)
    inv_rms = lax.rsqrt(jnp.mean(rows_float * rows_float, axis=-1, keepdims=True) + epsilon)
    return (rows_float, inv_rms, (rows_float * inv_rms).astype(BF16))


def finish(rows_float, inv_rms, incoming, grad_normed):
    grad_normed = grad_normed.astype(F32)
    inner = jnp.sum(grad_normed * rows_float, axis=-1, keepdims=True) / rows_float.shape[-1]
    grad_rows = inv_rms * grad_normed - inv_rms * inv_rms * inv_rms * rows_float * inner
    return (incoming.astype(F32) + grad_rows).astype(BF16)


def tn(a, b):
    return lax.dot_general(a, b, (((0,), (0,)), ((), ())), preferred_element_type=F32)


def nt(a, b):
    return lax.dot_general(a, b, (((1,), (1,)), ((), ())), preferred_element_type=F32)


def nn(a, b):
    return lax.dot_general(a, b, (((1,), (0,)), ((), ())), preferred_element_type=F32)


def kernel(
    width, group, tile,
    kept, sent, up, down,
    out_kept, out_sent, out_down,
    tok, outbox, rows, hidden, grad_pre, picks, weighted, pieces, back, ret, retin, upw, dnw, part, mirror,
    send_sem, recv_sem, local_sem,
):
    tiles = width // tile
    pipe, place = lax.axis_index("pipe"), lax.axis_index("expert")
    core, y, z = pipe % 2, place % NY, place // NY
    served = ((y + 1) // 2) % 2
    stay = core == served
    leave = core != served
    mine, other = 2 * z + y // 2, 2 * z + 1 - y // 2
    twin = (pipe + 1 - 2 * core, place)
    beside = (pipe, z * NY + y + 1 - 2 * (y % 2))
    opposite = (pipe, z * NY + 3 - y)
    above = (pipe, ((z + 1) % NZ) * NY + y)
    below = (pipe, ((z + NZ - 1) % NZ) * NY + y)
    crossed = (twin[0], beside[1])

    barrier = pltpu.get_barrier_semaphore()
    for device in (twin, beside, opposite, above, below):
        pl.semaphore_signal(barrier, inc=1, device_id=device, device_id_type=MESH)

    @pl.when(leave)
    def _():
        pl.semaphore_signal(barrier, inc=1, device_id=crossed, device_id_type=MESH)
        pl.semaphore_wait(barrier, 6)

    @pl.when(stay)
    def _():
        pl.semaphore_wait(barrier, 5)

    def remote(index, src, dst, device):
        return pltpu.make_async_remote_copy(
            src_ref=src, dst_ref=dst, send_sem=send_sem.at[index], recv_sem=recv_sem.at[index],
            device_id=device, device_id_type=MESH,
        )

    def mine_of(c):
        return pl.ds(2 * c * SLOTS, SLOTS)

    def other_of(c):
        return pl.ds((2 * c + 1) * SLOTS, SLOTS)

    first, second = pl.ds(0, TOK), pl.ds(TOK, TOK)
    copies = {
        UP_A: remote(UP_A, up, upw.at[0], crossed),
        DOWN_A: remote(DOWN_A, down, dnw.at[0], crossed),
        UP_B: remote(UP_B, upw.at[0], upw.at[1], twin),
        DOWN_B: remote(DOWN_B, dnw.at[0], dnw.at[1], twin),
    }
    NORMED, GRADS = 0, PARTS
    for part_of, of, packed_of in (
        (NORMED, pl.ds(0, PAD + width), pl.ds(0, width)),
        (GRADS, pl.ds(PAD + width, width), pl.ds(width, width)),
    ):
        for name, src, dst, device in (
            (KEPT_UP, kept.at[:, of], tok.at[1, first, of], above),
            (KEPT_DN, kept.at[:, of], tok.at[1, second, of], below),
            (SWAP, sent.at[:, of], tok.at[0, second, of], beside),
            (SWAPPED_UP, tok.at[0, second, of], tok.at[2, first, of], above),
            (SWAPPED_DN, tok.at[0, second, of], tok.at[2, second, of], below),
            (FAR_UP, tok.at[1, first, of], tok.at[3, first, of], above),
            (FAR_DN, tok.at[2, second, of], tok.at[3, second, of], below),
        ):
            copies[part_of + name] = remote(part_of + name, src, dst, device)
        for c in range(4):
            copies[part_of + PACKED + c] = remote(
                part_of + PACKED + c,
                outbox.at[pl.ds(c * SLOTS, SLOTS), packed_of], rows.at[other_of(c), packed_of], opposite,
            )
    whole_copies = []

    def start(*names):
        for name in names:
            copies[name].start()
            whole_copies.append(name)

    def arrived(*names):
        for name in names:
            copies[name].wait_recv()

    def columns(j, offset=0):
        return pl.ds(pl.multiple_of(offset + j * tile, 128), tile)

    def tiled(kind, j):
        where = columns(j)
        if kind >= BACK and kind < BACK + 4:
            c = kind - BACK
            src, dst, device = pieces.at[other_of(c), where], back.at[pl.ds(c * SLOTS, SLOTS), where], opposite
        elif kind == MIRROR:
            src, dst, device = part.at[:, where], mirror.at[:, where], twin
        elif kind == HOME:
            src, dst, device = mirror.at[:, where], out_down.at[:, where], crossed
        elif kind == RESULT:
            src, dst, device = ret.at[RESULT, :, where], out_sent.at[:, where], beside
        else:
            src, dst = ret.at[kind, :, where], retin.at[kind, :, where]
            device = above if kind in (SUM_FAR_SWAPPED, SUM_ABOVE_KEPT, SUM_ABOVE_SWAPPED) else below
        return remote(TILED + kind * tiles + j, src, dst, device)

    def loop(step):
        def body(j, carry):
            step(j)
            return carry

        lax.fori_loop(0, tiles, body, 0)

    def matrices(c):
        table = tok[c, :, pl.ds(0, PAD)].astype(F32)
        lane = lax.broadcasted_iota(jnp.int32, (PAIR, PAD), 1)
        later = jnp.where(lax.broadcasted_iota(jnp.int32, (PAIR, 1), 0) >= TOK, F32(CAP), F32(0.0))
        plain, gates = [], []
        for expert in (mine, other):
            gate = jnp.sum(jnp.where(lane == expert, table, 0.0), axis=1, keepdims=True)
            rank = jnp.sum(jnp.where(lane == expert + EXPERTS, table, 0.0), axis=1, keepdims=True) + later
            hit = (gate != 0.0) & (rank == lane.astype(F32))
            plain.append(jnp.where(hit, 1.0, 0.0).astype(BF16))
            gates.append(jnp.where(hit, gate, 0.0).astype(BF16))
        return jnp.concatenate(plain, axis=1), jnp.concatenate(gates, axis=1)

    def pack_part(c, matrix, offset):
        def step(j):
            where = columns(j, offset)
            got = tn(matrix, tok[c, :, columns(j, PAD + offset)]).astype(BF16)
            rows[mine_of(c), where] = got[:SLOTS]
            outbox[pl.ds(c * SLOTS, SLOTS), where] = got[PAD : PAD + SLOTS]

        loop(step)

    def pack_normed(c):
        plain, gates = matrices(c)
        picks[c] = plain
        weighted[c] = gates
        pack_part(c, plain, 0)
        start(NORMED + PACKED + c)

    def pack_grads(c):
        pack_part(c, weighted[c], width)
        start(GRADS + PACKED + c)

    def activate(c):
        block = pl.ds(2 * c * SLOTS, 2 * SLOTS)

        def half(g, carry):
            where = pl.ds(pl.multiple_of(g * group, group), group)
            pre = nn(rows[block, pl.ds(0, width)], upw[g])
            s = jax.nn.sigmoid(pre)
            hidden[block, where] = (pre * s).astype(BF16)
            grad_hidden = nt(rows[block, pl.ds(width, width)], dnw[g])
            grad_pre[block, where] = (grad_hidden * s * (1.0 + pre * (1.0 - s))).astype(BF16)
            return carry

        lax.fori_loop(0, 2, half, 0)

    def piece(c):
        block = pl.ds(2 * c * SLOTS, 2 * SLOTS)

        def step(j):
            where = columns(j)
            total = nt(grad_pre[block, pl.ds(0, group)], upw[0, where, :]) + nt(
                grad_pre[block, pl.ds(group, group)], upw[1, where, :]
            )
            total = total.astype(BF16)
            pieces[other_of(c), where] = total[SLOTS:]
            tiled(BACK + c, j).start()
            pieces[mine_of(c), where] = total[:SLOTS]

        loop(step)

    def scatter(c, half, extras, store, awaited):
        tokens = pl.ds(half * TOK, TOK)

        def step(j):
            where = columns(j)
            for kind in awaited + extras:
                tiled(kind, j).wait_recv()
            total = nn(picks[c, tokens, pl.ds(0, SLOTS)], pieces[mine_of(c), where])
            total += nn(picks[c, tokens, pl.ds(PAD, SLOTS)], back[pl.ds(c * SLOTS, SLOTS), where])
            for extra in extras:
                total += retin[extra, :, where].astype(F32)
            ret[store, :, where] = total.astype(BF16)
            if store <= RESULT:
                tiled(store, j).start()

        loop(step)

    start(NORMED + KEPT_UP, NORMED + KEPT_DN, NORMED + SWAP)
    own = pltpu.make_async_copy(kept, tok.at[0, first], local_sem.at[0])
    own.start()

    @pl.when(stay)
    def _():
        one = pltpu.make_async_copy(up, upw.at[0], local_sem.at[1])
        two = pltpu.make_async_copy(down, dnw.at[0], local_sem.at[2])
        one.start()
        two.start()
        one.wait()
        two.wait()
        copies[UP_B].start()
        copies[DOWN_B].start()

    arrived(NORMED + SWAP)
    start(NORMED + SWAPPED_UP, NORMED + SWAPPED_DN, GRADS + SWAP)
    own.wait()
    pack_normed(0)
    arrived(NORMED + KEPT_UP)
    start(NORMED + FAR_UP)
    arrived(NORMED + KEPT_DN)
    pack_normed(1)
    arrived(GRADS + SWAP)

    @pl.when(leave)
    def _():
        copies[UP_A].start()

    pack_grads(0)
    arrived(NORMED + SWAPPED_DN)
    start(NORMED + FAR_DN, GRADS + KEPT_DN)
    arrived(NORMED + SWAPPED_UP)
    start(GRADS + KEPT_UP)

    @pl.when(leave)
    def _():
        copies[DOWN_A].start()

    pack_normed(2)
    arrived(NORMED + FAR_UP)
    start(GRADS + SWAPPED_UP)
    arrived(NORMED + FAR_DN)
    start(GRADS + SWAPPED_DN)
    pack_normed(3)
    arrived(GRADS + KEPT_UP)
    start(GRADS + FAR_UP)
    arrived(GRADS + KEPT_DN)
    pack_grads(1)

    @pl.when(leave)
    def _():
        copies[UP_A].wait()
        copies[UP_B].start()

    arrived(GRADS + SWAPPED_DN)
    start(GRADS + FAR_DN)
    arrived(GRADS + SWAPPED_UP)
    pack_grads(2)

    @pl.when(leave)
    def _():
        copies[DOWN_A].wait()
        copies[DOWN_B].start()

    arrived(UP_B, DOWN_B)
    arrived(NORMED + PACKED + 1, GRADS + PACKED + 1)
    activate(1)
    piece(1)
    arrived(GRADS + FAR_UP, GRADS + FAR_DN)
    pack_grads(3)
    arrived(NORMED + PACKED, GRADS + PACKED)
    activate(0)
    arrived(NORMED + PACKED + 2, GRADS + PACKED + 2)
    activate(2)
    scatter(1, 1, (), SUM_ABOVE_KEPT, (BACK + 1,))
    arrived(NORMED + PACKED + 3, GRADS + PACKED + 3)
    piece(2)

    def gradient(j, g):
        return tn(hidden[:, pl.ds(g * group, group)], rows[:, columns(j, width)])

    def theirs(j):
        part[:, columns(j)] = gradient(j, 1).astype(BF16)
        tiled(MIRROR, j).start()

    def stays(j):
        return pltpu.make_async_copy(mirror.at[:, columns(j)], out_down.at[:, columns(j)], local_sem.at[3 + j])

    def ours(j):
        value = gradient(j, 0).astype(BF16).astype(F32)
        tiled(MIRROR, j).wait_recv()
        mirror[:, columns(j)] = (value + mirror[:, columns(j)].astype(F32)).astype(BF16)

        @pl.when(stay)
        def _():
            stays(j).start()

        @pl.when(leave)
        def _():
            tiled(HOME, j).start()

    activate(3)
    loop(theirs)
    piece(3)
    loop(ours)
    scatter(3, 0, (), SUM_FAR_KEPT, (BACK + 3,))
    scatter(3, 1, (), SUM_FAR_SWAPPED, ())
    piece(0)
    scatter(2, 0, (), SUM_BELOW_SWAPPED, (BACK + 2,))
    scatter(1, 0, (SUM_FAR_KEPT,), SUM_BELOW_KEPT, ())
    scatter(2, 1, (SUM_FAR_SWAPPED,), SUM_ABOVE_SWAPPED, ())
    scatter(0, 1, (SUM_BELOW_SWAPPED, SUM_ABOVE_SWAPPED), RESULT, (BACK,))
    scatter(0, 0, (SUM_ABOVE_KEPT, SUM_BELOW_KEPT), RESULT + 1, ())
    result = pltpu.make_async_copy(ret.at[RESULT + 1], out_kept, local_sem.at[0])
    result.start()

    for name in whole_copies + [UP_B, DOWN_B]:
        copies[name].wait_send()

    def ended(j):
        for kind in range(HOME):
            tiled(kind, j).wait_send()
        tiled(RESULT, j).wait_recv()

        @pl.when(stay)
        def _():
            stays(j).wait()

        @pl.when(leave)
        def _():
            tiled(HOME, j).wait()

    loop(ended)
    result.wait()


def exchange(kept, sent, up, down):
    width, group = up.shape
    tile = 512 if width % 512 == 0 else 128
    tiles = width // tile
    copies = TILED + TILED_KINDS * tiles
    return pl.pallas_call(
        functools.partial(kernel, width, group, tile),
        out_shape=[
            jax.ShapeDtypeStruct((TOK, width), BF16),
            jax.ShapeDtypeStruct((TOK, width), BF16),
            jax.ShapeDtypeStruct((group, width), BF16),
        ],
        in_specs=[pl.BlockSpec(memory_space=pl.ANY)] * 4,
        out_specs=[pl.BlockSpec(memory_space=pl.ANY)] * 3,
        scratch_shapes=[
            pltpu.VMEM((4, PAIR, 2 * width + PAD), BF16),
            pltpu.VMEM((4 * SLOTS, 2 * width), BF16),
            pltpu.VMEM((8 * SLOTS, 2 * width), BF16),
            pltpu.VMEM((8 * SLOTS, 2 * group), BF16),
            pltpu.VMEM((8 * SLOTS, 2 * group), BF16),
            pltpu.VMEM((4, PAIR, 2 * PAD), BF16),
            pltpu.VMEM((4, PAIR, 2 * PAD), BF16),
            pltpu.VMEM((8 * SLOTS, width), BF16),
            pltpu.VMEM((4 * SLOTS, width), BF16),
            pltpu.VMEM((8, TOK, width), BF16),
            pltpu.VMEM((6, TOK, width), BF16),
            pltpu.VMEM((2, width, group), BF16),
            pltpu.VMEM((2, group, width), BF16),
            pltpu.VMEM((group, width), BF16),
            pltpu.VMEM((group, width), BF16),
            pltpu.SemaphoreType.DMA((copies,)),
            pltpu.SemaphoreType.DMA((copies,)),
            pltpu.SemaphoreType.DMA((3 + tiles,)),
        ],
        compiler_params=pltpu.CompilerParams(
            collective_id=0, has_side_effects=True, vmem_limit_bytes=62 * 1024 * 1024
        ),
    )(kept, sent, up, down)


def on_device(fx, fg, froutes, flogits, rx, rg, rroutes, rlogits, up_weight, down_weight):
    core = lax.axis_index("pipe") % 2
    y = lax.axis_index("expert") % NY
    front_stays = core == (y + 1) // 2 % 2
    both = []
    for x, g, routes, logits in ((fx, fg, froutes, flogits), (rx, rg, rroutes, rlogits)):
        rows_float, inv_rms, normed = normalize(x[0])
        gates = gate_table(routes[0], logits[0])
        chosen = (gates != 0).astype(jnp.int32)
        rank = (jnp.cumsum(chosen, axis=0) - chosen).astype(BF16)
        table = jnp.pad(jnp.concatenate([gates, rank], axis=1), ((0, 0), (0, PAD - 2 * EXPERTS)))
        both.append((rows_float, inv_rms, g[0], jnp.concatenate([table, normed, g[0]], axis=1)))
    kept = jnp.where(front_stays, both[0][3], both[1][3])
    sent = jnp.where(front_stays, both[1][3], both[0][3])
    from_kept, from_sent, down_grad = exchange(kept, sent, up_weight[0], down_weight[0])
    results = []
    for stays, (rows_float, inv_rms, g, _) in zip((front_stays, ~front_stays), both):
        results.append(finish(rows_float, inv_rms, g, jnp.where(stays, from_kept, from_sent)))
    return (results[0][None], results[1][None], down_grad[None])


def solution(mesh):
    rows = P("pipe", "expert", None)
    return jax.shard_map(
        on_device,
        mesh=mesh,
        in_specs=(rows,) * 8 + (P("pipe", None, "expert"), rows),
        out_specs=(rows, rows, rows),
        check_vma=False,
    )
```

time: 292 us -> 249 us (0.85)
  Pallas kernels: 276 us -> 236 us
  other arithmetic: 12.1 us -> 9.15 us
    pallas_call x1, Pallas kernels: 276 us -> 236 us  [exchange(): pl.pallas_call(functools.partial(kernel, width, group, tile), out_shape=[...]
where the time goes in v1:
time: 249 us
  Pallas kernels  236 us (95%)
  other arithmetic  9.15 us (4%)
  local copies, waits for them, and re-layouts  2.8 us (1%)
    pallas_call x1, Pallas kernels, exchange(): pl.pallas_call(functools.partial(kernel, width, group, tile), out_shape=[...  236 us

profile of v1, /device:TPU:36, one launch (start us, length us, event | category | flops | bytes accessed | tf_op | source)
XLA Modules:
  0.0 248.6 jit_solution(13406810045266893592)
XLA Ops:
  0.6 0.0 copy-start.5
  0.6 0.0 copy-start.9
  0.7 0.0 copy-start.7
  0.7 0.0 copy-start.10
  0.7 0.0 copy-start.8
  0.7 0.0 copy-start.6
  0.8 1.3 fusion.6
  2.1 1.2 fusion.10
  3.3 1.4 fusion.7
  4.7 0.0 copy-done.9
  4.8 0.0 copy-done.7
  4.8 0.1 copy.27
  4.9 0.1 reduce_window_sum.17
  5.0 0.0 copy-done.10
  5.1 0.1 copy.28
  5.2 0.1 reduce_window_sum.18
  5.3 0.1 fusion.20
  5.4 1.5 broadcast_select_fusion
  7.0 235.7 %shard_map.121 = (bf16[64,3584]{1,0:T(8,128)(2,1)}, bf16[64,3584]{1,0:T(8,128)(2,1)}, bf16[512,3584]{1,0:T(8,128)(2,1)}) custom-call(bf16[64,7296]{1,0:T(8,128)(2,1)} %get-tuple-element.12.kept, bf16[64,7296]{1,0:T(8,128)(2,1)} %get-tuple-element.11.sent, bf16[3584,512]{1,0:T(8,128)(2,1)} %bitcast.47, bf16[512,3584]{1,0:T(8,128)(2,1)} %bitcast.48), custom_call_target="tpu_custom_call" | custom-call | tf_op jit(solution)/shard_map/pallas_call | solution.py:400
  242.7 1.6 fusion.13
  244.4 0.0 copy-start.2
  244.4 1.6 fusion.14
  246.0 0.7 copy-done.2
  246.7 1.8 copy.30
  (25 shorter events, 0.2 us)
Async XLA Ops:
  0.6 4.8 %copy-start.5 = (bf16[1,64,3584]{2,1,0:T(8,128)(2,1)S(1)}, bf16[1,64,3584]{2,1,0:T(8,128)(2,1)}, u32[]{:S(2)}) copy-start(bf16[1,64,3584]{2,1,0:T(8,128)(2,1)} %param.15) | copy-start | bytes 1376260
  0.6 4.1 %copy-start.9 = (bf16[1,64,4]{1,2,0:T(4,128)(2,1)S(1)}, bf16[1,64,4]{1,2,0:T(4,128)(2,1)}, u32[]{:S(2)}) copy-start(bf16[1,64,4]{1,2,0:T(4,128)(2,1)} %param.13) | copy-start | bytes 1540
  0.7 4.1 %copy-start.7 = (s32[1,64,4]{1,2,0:T(4,128)S(1)}, s32[1,64,4]{1,2,0:T(4,128)}, u32[]{:S(2)}) copy-start(s32[1,64,4]{1,2,0:T(4,128)} %param.12) | copy-start | bytes 3076
  0.7 4.4 %copy-start.10 = (bf16[1,64,4]{1,2,0:T(4,128)(2,1)S(1)}, bf16[1,64,4]{1,2,0:T(4,128)(2,1)}, u32[]{:S(2)}) copy-start(bf16[1,64,4]{1,2,0:T(4,128)(2,1)} %param.17) | copy-start | bytes 1540
  0.7 4.4 %copy-start.8 = (s32[1,64,4]{1,2,0:T(4,128)S(1)}, s32[1,64,4]{1,2,0:T(4,128)}, u32[]{:S(2)}) copy-start(s32[1,64,4]{1,2,0:T(4,128)} %param.16) | copy-start | bytes 3076
  0.7 4.7 %copy-start.6 = (bf16[1,64,3584]{2,1,0:T(8,128)(2,1)S(1)}, bf16[1,64,3584]{2,1,0:T(8,128)(2,1)}, u32[]{:S(2)}) copy-start(bf16[1,64,3584]{2,1,0:T(8,128)(2,1)} %param.11) | copy-start | bytes 1376260
  7.0 235.7 %copy-start = (bf16[1,64,3584]{2,1,0:T(8,128)(2,1)S(1)}, bf16[1,64,3584]{2,1,0:T(8,128)(2,1)}, u32[]{:S(2)}) copy-start(bf16[1,64,3584]{2,1,0:T(8,128)(2,1)} %param.14) | copy-start | bytes 1376260
  7.0 235.7 %copy-start.1 = (bf16[1,64,3584]{2,1,0:T(8,128)(2,1)S(1)}, bf16[1,64,3584]{2,1,0:T(8,128)(2,1)}, u32[]{:S(2)}) copy-start(bf16[1,64,3584]{2,1,0:T(8,128)(2,1)} %param.10) | copy-start | bytes 1376260
  242.7 1.7 copy-start.3
  242.7 1.7 copy-start.4
  244.4 2.4 copy-start.2

commit v2 on v1

--- a/solution.py
+++ b/solution.py
@@ -394,7 +394,7 @@
 
 def exchange(kept, sent, up, down):
     width, group = up.shape
-    tile = 512 if width % 512 == 0 else 128
+    tile = 896 if width % 896 == 0 else 128
     tiles = width // tile
     copies = TILED + TILED_KINDS * tiles
     return pl.pallas_call(

time: 249 us -> 247 us (level)
  no operation moved by 1% of the time
where the time goes in v2:
time: 247 us; the launch traced here: 246 us
  Pallas kernels  234 us (95%)
  other arithmetic  9.15 us (4%)
  local copies, waits for them, and re-layouts  2.8 us (1%)
    pallas_call x1, Pallas kernels, exchange(): pl.pallas_call(functools.partial(kernel, width, group, tile), out_shape=[...  234 us

profile of v2, /device:TPU:36, one launch (start us, length us, event | category | flops | bytes accessed | tf_op | source)
XLA Modules:
  0.0 246.4 jit_solution(259876944769454851)
XLA Ops:
  0.6 0.0 copy-start.5
  0.6 0.0 copy-start.9
  0.7 0.0 copy-start.7
  0.7 0.0 copy-start.10
  0.7 0.0 copy-start.8
  0.7 0.0 copy-start.6
  0.8 1.3 fusion.6
  2.1 1.2 fusion.10
  3.3 1.4 fusion.7
  4.7 0.0 copy-done.9
  4.8 0.0 copy-done.7
  4.8 0.1 copy.27
  4.9 0.1 reduce_window_sum.17
  5.1 0.1 copy.28
  5.2 0.1 reduce_window_sum.18
  5.3 0.1 fusion.20
  5.4 1.5 broadcast_select_fusion
  7.0 233.6 %shard_map.121 = (bf16[64,3584]{1,0:T(8,128)(2,1)}, bf16[64,3584]{1,0:T(8,128)(2,1)}, bf16[512,3584]{1,0:T(8,128)(2,1)}) custom-call(bf16[64,7296]{1,0:T(8,128)(2,1)} %get-tuple-element.12.kept, bf16[64,7296]{1,0:T(8,128)(2,1)} %get-tuple-element.11.sent, bf16[3584,512]{1,0:T(8,128)(2,1)} %bitcast.47, bf16[512,3584]{1,0:T(8,128)(2,1)} %bitcast.48), custom_call_target="tpu_custom_call" | custom-call | tf_op jit(solution)/shard_map/pallas_call | solution.py:400
  240.6 0.0 copy-done
  240.6 0.0 copy-done.1
  240.6 1.6 fusion.13
  242.3 1.6 fusion.14
  243.9 0.7 copy-done.2
  244.6 1.8 copy.30
  (25 shorter events, 0.2 us)
Async XLA Ops:
  0.6 4.8 %copy-start.5 = (bf16[1,64,3584]{2,1,0:T(8,128)(2,1)S(1)}, bf16[1,64,3584]{2,1,0:T(8,128)(2,1)}, u32[]{:S(2)}) copy-start(bf16[1,64,3584]{2,1,0:T(8,128)(2,1)} %param.15) | copy-start | bytes 1376260
  0.6 4.1 %copy-start.9 = (bf16[1,64,4]{1,2,0:T(4,128)(2,1)S(1)}, bf16[1,64,4]{1,2,0:T(4,128)(2,1)}, u32[]{:S(2)}) copy-start(bf16[1,64,4]{1,2,0:T(4,128)(2,1)} %param.13) | copy-start | bytes 1540
  0.7 4.1 %copy-start.7 = (s32[1,64,4]{1,2,0:T(4,128)S(1)}, s32[1,64,4]{1,2,0:T(4,128)}, u32[]{:S(2)}) copy-start(s32[1,64,4]{1,2,0:T(4,128)} %param.12) | copy-start | bytes 3076
  0.7 4.4 %copy-start.10 = (bf16[1,64,4]{1,2,0:T(4,128)(2,1)S(1)}, bf16[1,64,4]{1,2,0:T(4,128)(2,1)}, u32[]{:S(2)}) copy-start(bf16[1,64,4]{1,2,0:T(4,128)(2,1)} %param.17) | copy-start | bytes 1540
  0.7 4.4 %copy-start.8 = (s32[1,64,4]{1,2,0:T(4,128)S(1)}, s32[1,64,4]{1,2,0:T(4,128)}, u32[]{:S(2)}) copy-start(s32[1,64,4]{1,2,0:T(4,128)} %param.16) | copy-start | bytes 3076
  0.7 4.7 %copy-start.6 = (bf16[1,64,3584]{2,1,0:T(8,128)(2,1)S(1)}, bf16[1,64,3584]{2,1,0:T(8,128)(2,1)}, u32[]{:S(2)}) copy-start(bf16[1,64,3584]{2,1,0:T(8,128)(2,1)} %param.11) | copy-start | bytes 1376260
  7.0 233.6 %copy-start = (bf16[1,64,3584]{2,1,0:T(8,128)(2,1)S(1)}, bf16[1,64,3584]{2,1,0:T(8,128)(2,1)}, u32[]{:S(2)}) copy-start(bf16[1,64,3584]{2,1,0:T(8,128)(2,1)} %param.14) | copy-start | bytes 1376260
  7.0 233.6 %copy-start.1 = (bf16[1,64,3584]{2,1,0:T(8,128)(2,1)S(1)}, bf16[1,64,3584]{2,1,0:T(8,128)(2,1)}, u32[]{:S(2)}) copy-start(bf16[1,64,3584]{2,1,0:T(8,128)(2,1)} %param.10) | copy-start | bytes 1376260
  240.6 1.7 copy-start.3
  240.6 1.7 copy-start.4
  242.2 2.4 copy-start.2
